TPU v7x, 32 devices: a whole 2x2x4 slice. The times are simulated.
32 devices in a mesh: row: 8 (over y, x, core), col: 4 (over z).
Axes of the slice: x: 2, y: 2, z: 4, core: 2. Of those that a mesh axis runs over, the one named last changes fastest.
Arguments:
- b_ingest: bfloat16 [65536, 1024], P(('row', 'col')), may hold values from -6 to 6
- source_point: int32 [65536], P(('row', 'col')), may hold values from 0 to 65535, as said below
- panels: bfloat16 [2, 8, 8, 1024, 1024], P(None, None, 'row', 'col'), may hold values from -0.1875 to 0.1875
- diag_inverse: bfloat16 [2, 1024, 1024], replicated, may hold values from -1 to 1.5, as said below
Outputs:
- updated: bfloat16 [8, 8, 1024, 1024], P(None, 'row', 'col')
Inputs may be any that keep to these rules, and one draw needn't show every extreme that they name: source_point is a permutation of 0 to 65535. Say point i lies in block b = i // 1024 at offset o = i mod 1024; it belongs to the device with row index b mod 8 and col index o // (1024 / 4). The shard of source_point on each device along row+col holds exactly 64 points of every device. diag_inverse[k] is lower triangular with diagonal entries between 0.5 and 1.5.
All inputs are finite; a program needn't handle non-finite values.
Results may differ from a plain program's by a relative error of at most 0.0056.
Values may be sent and summed in bfloat16 or wider, within the bound.
A program may use at most 64 MiB of HBM per device.

v0:
```python
import jax
import jax.numpy as jnp
from jax import lax
from jax.sharding import PartitionSpec as P


def broadcast(block, axis, owner):
    block = jnp.where(lax.axis_index(axis) == owner, block, jnp.zeros_like(block))
    return lax.psum(block, axis)


def per_device(b_ingest, source_point, panels, diag_inverse):
    row_count = lax.axis_size("row")
    col_count = lax.axis_size("col")
    dev_count = row_count * col_count
    block_rows = panels.shape[3]
    panel_width = panels.shape[4]
    local_count = panels.shape[1]
    rows_dev = local_count * block_rows
    draw_count = b_ingest.shape[1]
    per_peer = rows_dev // dev_count
    owner_block = source_point // panel_width
    target = owner_block % row_count * col_count + source_point % panel_width // block_rows
    sort_keys = target * rows_dev + jnp.arange(rows_dev, dtype=jnp.int32)
    ordering = jnp.argsort(sort_keys)
    ordered = b_ingest[ordering]
    ordered_ids = source_point[ordering]
    arrived, arrived_ids = (
        lax.all_to_all(
            ordered.reshape(dev_count, per_peer, draw_count),
            ("row", "col"),
            split_axis=0,
            concat_axis=0,
            tiled=True,
        ),
        lax.all_to_all(
            ordered_ids.reshape(dev_count, per_peer),
            ("row", "col"),
            split_axis=0,
            concat_axis=0,
            tiled=True,
        ),
    )
    arrived = arrived.reshape(rows_dev, draw_count)
    arrived_ids = arrived_ids.reshape(rows_dev)
    arrived_block = arrived_ids // panel_width
    local_row = arrived_block // row_count * block_rows + arrived_ids % panel_width % block_rows
    resident = jnp.zeros((rows_dev, draw_count), jnp.bfloat16).at[local_row].set(arrived)
    running = resident.astype(jnp.float32)
    row_id = lax.axis_index("row")
    col_id = lax.axis_index("col")
    global_block = jnp.arange(rows_dev, dtype=jnp.int32) // block_rows * row_count + row_id
    solved = []
    for panel_index in range(2):
        factor_rows = panels[panel_index].reshape(rows_dev, panel_width)
        inverse = diag_inverse[panel_index]
        leading = running[:block_rows].astype(jnp.bfloat16)
        shared = broadcast(leading, "row", panel_index)
        full_solved = jnp.dot(
            inverse,
            lax.all_gather(shared, "col", axis=0, tiled=True),
            preferred_element_type=jnp.float32,
        ).astype(jnp.bfloat16)
        update = jnp.dot(factor_rows, full_solved, preferred_element_type=jnp.float32)
        own_solved = lax.dynamic_slice_in_dim(full_solved, col_id * block_rows, block_rows, 0)
        running = running - jnp.where((global_block > panel_index)[:, None], update, 0.0)
        solved.append(own_solved)
    result = running.astype(jnp.bfloat16)
    head_rows = result[:block_rows]
    head_rows = jnp.where(row_id == 0, solved[0], jnp.where(row_id == 1, solved[1], head_rows))
    result = jnp.concatenate([head_rows, result[block_rows:]], axis=0)
    return result.reshape(local_count, 1, block_rows, draw_count)


def solution(mesh):
    return jax.shard_map(
        per_device,
        mesh=mesh,
        in_specs=(
            P(("row", "col"), None),
            P(("row", "col")),
            P(None, None, "row", "col", None),
            P(),
        ),
        out_specs=P(None, "row", "col", None),
        check_vma=False,
    )
```

profile of v0, /device:TPU:11, one launch (start us, length us, event | category | flops | bytes accessed | tf_op | source)
XLA Modules:
  0.0 392.2 jit_solution(7554376530686336992)
XLA Ops:
  6.5 0.8 fusion.22
  7.3 5.0 %sort.17 = (s32[2048]{0:T(1024)}, s32[2048]{0:T(1024)S(1)}) sort(s32[2048]{0:T(1024)S(1)} %fusion.22, s32[2048]{0:T(1024)S(1)} %iota.15), dimensions={0}, to_apply=%region_0.1 | sort | flops 22528 | bytes 32768 | tf_op jit(solution)/shard_map/jit(argsort)/sort | solution.py:25
  12.4 11.8 %gather_fusion = s32[2048]{0:T(1024)S(1)} fusion(s32[2048]{0:T(1024)S(1)} %copy-done, s32[2048]{0:T(1024)S(1)} %fusion.30), kind=kCustom, calls=%fused_computation | custom fusion | bytes 24576 | tf_op jit(solution)/shard_map/gather | solution.py:27
  24.2 0.7 all_to_all.9
  24.9 6.3 %all-to-all-start = ((s32[32,1,64]{2,1,0:T(1,128)}), s32[32,1,64]{2,1,0:T(1,128)S(1)}, u32[]{:S(2)}, u32[]{:S(2)}) async-start(s32[32,1,64]{2,1,0:T(1,128)} %all_to_all.9), calls=%async_computation | async-start | bytes 32768 | tf_op jit(solution)/shard_map/all_to_all | solution.py:36
  31.2 13.7 %gather_fusion.1 = bf16[2048,1024]{1,0:T(8,128)(2,1)} fusion(bf16[2048,1024]{1,0:T(8,128)(2,1)} %param.4, s32[2048]{0:T(1024)S(1)} %fusion.30), kind=kCustom, calls=%fused_computation.1 | custom fusion | bytes 8396800 | tf_op jit(solution)/shard_map/gather | solution.py:26
  44.9 5.9 %all-to-all-start.1 = ((bf16[32,64,1024]{2,1,0:T(8,128)(2,1)}), bf16[32,64,1024]{2,1,0:T(8,128)(2,1)}, u32[]{:S(2)}, u32[]{:S(2)}) async-start(bf16[32,64,1024]{2,1,0:T(8,128)(2,1)} %bitcast.34), calls=%async_computation.1 | async-start | bytes 8388608 | tf_op jit(solution)/shard_map/all_to_all | solution.py:29
  50.8 0.0 all-reduce.3.cloned.1.call-start
  50.8 0.6 broadcast.322
  51.4 0.7 reduce.3
  52.1 0.1 reshape.224
  52.2 0.1 compare_select_fusion
  52.3 91.0 %all-to-all-done.1 = bf16[32,64,1024]{2,1,0:T(8,128)(2,1)} async-done(((bf16[32,64,1024]{2,1,0:T(8,128)(2,1)}), bf16[32,64,1024]{2,1,0:T(8,128)(2,1)}, u32[]{:S(2)}, u32[]{:S(2)}) %all-to-all-start.1) | async-done | bytes 4194336 | tf_op jit(solution)/shard_map/all_to_all | solution.py:29
  143.3 13.1 %scatter_custom_fusion = bf16[2048,1024]{1,0:T(8,128)(2,1)} fusion(s32[2048]{0:T(1024)S(1)} %bitcast.37, bf16[2048,1024]{1,0:T(8,128)(2,1)} %bitcast.2, bf16[]{:T(256)} %constant.99.clone.1), kind=kCustom, calls=%fused_computation.13 | custom fusion | bytes 4194816 | tf_op jit(solution)/shard_map/scatter | solution.py:48
  156.4 1.9 slice_select_fusion.1
  158.4 52.9 %all-reduce.3.cloned.1.call-done = bf16[256,1024]{1,0:T(8,128)(2,1)} async-done(((bf16[256,1024]{1,0:T(8,128)(2,1)}), bf16[256,1024]{1,0:T(8,128)(2,1)}) %all-reduce.3.cloned.1.call-update) | async-done | bytes 524304 | tf_op jit(solution)/shard_map/psum | solution.py:9
  211.3 0.2 all-reduce.5.cloned.1.call-start
  211.6 5.9 %fusion.35 = (bf16[1,8,1,256,1024]{4,3,2,1,0:T(8,128)(2,1)}, bf16[1,8,1,256,1024]{4,3,2,1,0:T(8,128)(2,1)}) fusion(bf16[2,8,1,256,1024]{4,3,2,1,0:T(8,128)(2,1)} %param.6), kind=kLoop, calls=%fused_computation.72 | loop fusion | bytes 16777216 | tf_op jit(solution)/shard_map/slice | solution.py:55
  217.5 40.7 %all-gather.3.cloned.1.call-done = bf16[1024,1024]{1,0:T(8,128)(2,1)} async-done(((bf16[256,1024]{1,0:T(8,128)(2,1)}), bf16[1024,1024]{1,0:T(8,128)(2,1)}) %all-gather.3.cloned.1.call-update) | async-done | bytes 2097168 | tf_op jit(solution)/shard_map/all_gather | solution.py:61
  258.2 4.7 %fusion.9 = bf16[1024,1024]{0,1:T(8,128)(2,1)S(1)} fusion(bf16[1024,1024]{1,0:T(8,128)(2,1)} %all-gather.3.cloned.1.call-done, bf16[2,1024,1024]{2,1,0:T(8,128)(2,1)} %param.7), kind=kOutput, calls=%fused_computation.15 | convolution fusion | flops 2148532224 | bytes 6291456 | tf_op jit(solution)/shard_map/dot_general | solution.py:59
  262.9 4.8 %bitcast_subtract_fusion.1 = f32[2048,1024]{1,0:T(8,128)S(1)} fusion(bf16[2048,1024]{1,0:T(8,128)(2,1)S(1)} %copy-done.1, pred[2048]{0:T(1024)(128)(4,1)S(1)} %fusion.29, bf16[2048,1024]{1,0:T(8,128)(2,1)S(1)} %bitcast.36, bf16[1024,1024]{0,1:T(8,128)(2,1)S(1)} %fusion.9), kind=kOutput, calls=%fused_computation.5 | convolution fusion | flops 4301258752 | bytes 18876416 | tf_op jit(solution)/shard_map/dot_general | solution.py:64
  267.7 3.2 copy-done.4
  270.9 0.8 fusion.15
  271.8 0.0 all-gather.5.cloned.1.call-start
  271.9 53.4 %all-reduce.5.cloned.1.call-done = bf16[256,1024]{1,0:T(8,128)(2,1)} async-done(((bf16[256,1024]{1,0:T(8,128)(2,1)}), bf16[256,1024]{1,0:T(8,128)(2,1)}) %all-reduce.5.cloned.1.call-update) | async-done | bytes 524304 | tf_op jit(solution)/shard_map/psum | solution.py:9
  325.3 46.7 %all-gather.5.cloned.1.call-done = bf16[1024,1024]{1,0:T(8,128)(2,1)} async-done(((bf16[256,1024]{1,0:T(8,128)(2,1)}), bf16[1024,1024]{1,0:T(8,128)(2,1)}) %all-gather.5.cloned.1.call-update) | async-done | bytes 2097168 | tf_op jit(solution)/shard_map/all_gather | solution.py:61
  371.9 4.7 %fusion.12 = bf16[1024,1024]{0,1:T(8,128)(2,1)S(1)} fusion(bf16[1024,1024]{1,0:T(8,128)(2,1)} %all-gather.5.cloned.1.call-done, bf16[2,1024,1024]{2,1,0:T(8,128)(2,1)} %param.7), kind=kOutput, calls=%fused_computation.16 | convolution fusion | flops 2148532224 | bytes 6291456 | tf_op jit(solution)/shard_map/dot_general | solution.py:59
  376.7 1.2 copy-done.5
  377.9 4.7 %fusion = bf16[2048,1024]{1,0:T(8,128)(2,1)S(1)} fusion(f32[2048,1024]{1,0:T(8,128)S(1)} %copy-done.5, pred[2048]{0:T(1024)(128)(4,1)S(1)} %fusion.28, bf16[2048,1024]{1,0:T(8,128)(2,1)S(1)} %bitcast.35, bf16[1024,1024]{0,1:T(8,128)(2,1)S(1)} %fusion.12), kind=kOutput, calls=%fused_computation.4 | convolution fusion | flops 4301258752 | bytes 18876416 | tf_op jit(solution)/shard_map/dot_general | solution.py:64
  382.6 0.4 slice.41
  382.9 0.3 fusion.16
  383.2 2.5 pad_maximum_fusion
  (20 shorter events, 0.2 us)
Async XLA Ops:
  6.5 5.9 %copy-start = (s32[2048]{0:T(1024)S(1)}, s32[2048]{0:T(1024)}, u32[]{:S(2)}) copy-start(s32[2048]{0:T(1024)} %param.5) | copy-start | bytes 24580
  24.9 20.0 %all-to-all-start = ((s32[32,1,64]{2,1,0:T(1,128)}), s32[32,1,64]{2,1,0:T(1,128)S(1)}, u32[]{:S(2)}, u32[]{:S(2)}) async-start(s32[32,1,64]{2,1,0:T(1,128)} %all_to_all.9), calls=%async_computation | async-start | bytes 32768 | tf_op jit(solution)/shard_map/all_to_all | solution.py:36
  44.9 98.5 %all-to-all-start.1 = ((bf16[32,64,1024]{2,1,0:T(8,128)(2,1)}), bf16[32,64,1024]{2,1,0:T(8,128)(2,1)}, u32[]{:S(2)}, u32[]{:S(2)}) async-start(bf16[32,64,1024]{2,1,0:T(8,128)(2,1)} %bitcast.34), calls=%async_computation.1 | async-start | bytes 8388608 | tf_op jit(solution)/shard_map/all_to_all | solution.py:29
  50.8 160.5 %all-reduce.3.cloned.1.call-start = ((), (), s32[]{:S(2)}) async-start(), calls=%async_computation.2 | async-start | bytes 1048576 | tf_op jit(solution)/shard_map/psum | solution.py:9
  158.3 99.9 %all-gather.3.cloned.1.call-start = ((), (), s32[]{:S(2)}) async-start(), calls=%async_computation.3 | async-start | bytes 2621440 | tf_op jit(solution)/shard_map/all_gather | solution.py:61
  211.3 113.9 %all-reduce.5.cloned.1.call-start = ((), (), s32[]{:S(2)}) async-start(), calls=%async_computation.4 | async-start | bytes 1048576 | tf_op jit(solution)/shard_map/psum | solution.py:9
  258.2 4.7 %copy-start.1 = (bf16[2048,1024]{1,0:T(8,128)(2,1)S(1)}, bf16[2048,1024]{1,0:T(8,128)(2,1)}, u32[]{:S(2)}) copy-start(bf16[2048,1024]{1,0:T(8,128)(2,1)} %scatter_custom_fusion) | copy-start | bytes 12582916
  258.2 4.7 %copy-start.3 = (bf16[1,8,1,256,1024]{4,3,2,1,0:T(8,128)(2,1)S(1)}, bf16[1,8,1,256,1024]{4,3,2,1,0:T(8,128)(2,1)}, u32[]{:S(2)}) copy-start(bf16[1,8,1,256,1024]{4,3,2,1,0:T(8,128)(2,1)} %get-tuple-element.8) | copy-start | bytes 12582916
  267.7 3.2 copy-start.4
  271.8 100.1 %all-gather.5.cloned.1.call-start = ((), (), s32[]{:S(2)}) async-start(), calls=%async_computation.5 | async-start | bytes 2621440 | tf_op jit(solution)/shard_map/all_gather | solution.py:61
  371.9 4.7 %copy-start.2 = (bf16[1,8,1,256,1024]{4,3,2,1,0:T(8,128)(2,1)S(1)}, bf16[1,8,1,256,1024]{4,3,2,1,0:T(8,128)(2,1)}, u32[]{:S(2)}) copy-start(bf16[1,8,1,256,1024]{4,3,2,1,0:T(8,128)(2,1)} %get-tuple-element.7) | copy-start | bytes 12582916
  371.9 5.9 %copy-start.5 = (f32[2048,1024]{1,0:T(8,128)S(1)}, f32[2048,1024]{1,0:T(8,128)}, u32[]{:S(2)}) copy-start(f32[2048,1024]{1,0:T(8,128)} %copy-done.4) | copy-start | bytes 25165828
Sparse Core Ops, SparseCore 0:
  158.5 52.7 all-reduce.2
  212.9 45.2 all-gather.2
  271.9 53.2 all-reduce.4
  326.7 45.2 all-gather.4
where the time goes:
time: 396 us; the launch traced here: 392 us
  waiting for transfers between devices  285 us (72%)
  local copies, waits for them, and re-layouts  50.6 us (13%)
  matrix products  18.9 us (5%)
  between operations  13.3 us (3%)
  starting transfers between devices  12.6 us (3%)
  other arithmetic  12.1 us (3%)
    psum x2, waiting for transfers between devices, broadcast(): return lax.psum(block, axis)  106 us
    all_to_all x1, waiting for transfers between devices, per_device(): lax.all_to_all(ordered.reshape(dev_count, per_peer, draw_count), ('row',...  91 us
    all_gather x2, waiting for transfers between devices, per_device(): lax.all_gather(shared, 'col', axis=0, tiled=True)  87.4 us
    gather x1, local copies, waits for them, and re-layouts, per_device(): ordered = b_ingest[ordering]  13.7 us
    scatter x1, local copies, waits for them, and re-layouts, per_device(): jnp.zeros((rows_dev, draw_count), jnp.bfloat16).at[local_row].set(arrived)  13.1 us
    gather x1, local copies, waits for them, and re-layouts, per_device(): ordered_ids = source_point[ordering]  11.8 us
    dot_general x2, matrix products, per_device(): jnp.dot(factor_rows, full_solved, preferred_element_type=jnp.float32)  9.48 us
    dot_general x2, matrix products, per_device(): jnp.dot(inverse, lax.all_gather(shared, 'col', axis=0, tiled=True), prefe...  9.39 us
  transfers between devices with their start and end apart: 6, of which 5 were waited for; matrix products, arithmetic and copies ran while one was open for 5% of the time, Pallas kernels for 0%

commit v1 on v0

--- a/solution.py
+++ b/solution.py
@@ -1,7 +1,16 @@
+import functools
+
 import jax
 import jax.numpy as jnp
 from jax import lax
+from jax.experimental import pallas as pl
+from jax.experimental.pallas import tpu as pltpu
 from jax.sharding import PartitionSpec as P
+
+MESH = pl.DeviceIdType.MESH
+BF16 = jnp.bfloat16
+F32 = jnp.float32
+GROUP = 256
 
 
 def broadcast(block, axis, owner):
@@ -9,7 +18,7 @@
     return lax.psum(block, axis)
 
 
-def per_device(b_ingest, source_point, panels, diag_inverse):
+def plain_per_device(b_ingest, source_point, panels, diag_inverse):
     row_count = lax.axis_size("row")
     col_count = lax.axis_size("col")
     dev_count = row_count * col_count
@@ -72,6 +81,349 @@
     return result.reshape(local_count, 1, block_rows, draw_count)
 
 
+def dot(a, b):
+    return jnp.dot(a, b, preferred_element_type=F32)
+
+
+def kernel(
+    R, C, panel_width, id_ref, b_ref, pan_hbm, diag_hbm, out_ref,
+    bs, rv, ids_s, ids_r, rank_ref, lr_ref, pan, dg, H, sol, acc,
+    local_sem, self_sem, s_send, s_recv, i_send, i_recv, a_send, b_send, c_send, d_send, p_recv, d_recv,
+):
+    D = R * C
+    rows_dev, draws = b_ref.shape
+    per_peer = rows_dev // D
+    L = pan.shape[1]
+    block_rows = pan.shape[2]
+    nq = R // 2
+    sub = block_rows // nq
+    in_group = GROUP // per_peer
+    groups = rows_dev // GROUP
+    row = lax.axis_index("row")
+    col = lax.axis_index("col")
+    me = row * C + col
+    core = lax.rem(row, 2)
+    quarter = lax.div(row, 2)
+    sibling = row + 1 - 2 * core
+
+    pan_copy = pltpu.make_async_copy(pan_hbm.at[:, :, 0], pan, local_sem.at[0])
+    diag_copy = pltpu.make_async_copy(diag_hbm, dg, local_sem.at[1])
+    pan_copy.start()
+    diag_copy.start()
+
+    barrier = pltpu.get_barrier_semaphore()
+
+    def greet(i, _):
+        peer = lax.rem(me + i, D)
+        pl.semaphore_signal(barrier, inc=1, device_id=(lax.div(peer, C), lax.rem(peer, C)), device_id_type=MESH)
+        return 0
+
+    lax.fori_loop(1, D, greet, 0)
+
+    ids = id_ref[...]
+    block = lax.div(ids, panel_width)
+    offset = ids - block * panel_width
+    local_block = lax.div(block, R)
+    target_col = lax.div(offset, block_rows)
+    target = (block - local_block * R) * C + target_col
+    local_row = local_block * block_rows + offset - target_col * block_rows
+    hits = jnp.where(lax.broadcasted_iota(jnp.int32, (D, rows_dev), 0) == target, 1.0, 0.0)
+    chunks = [hits[:, g * GROUP:(g + 1) * GROUP] for g in range(groups)]
+    upper = jnp.where(
+        lax.broadcasted_iota(jnp.int32, (GROUP, GROUP), 0) < lax.broadcasted_iota(jnp.int32, (GROUP, GROUP), 1), 1.0, 0.0
+    ).astype(BF16)
+    before = dot(jnp.concatenate(chunks, axis=0).astype(BF16), upper)
+    carry = jnp.zeros((D, 1), F32)
+    for g in range(groups):
+        part = chunks[g] * (before[g * D:(g + 1) * D] + carry)
+        rank_ref[:, g * GROUP:(g + 1) * GROUP] = jnp.sum(part, axis=0, keepdims=True).astype(jnp.int32)
+        carry = carry + jnp.sum(chunks[g], axis=1, keepdims=True)
+    rank = rank_ref[...]
+    place = target * per_peer + rank
+    high = lax.div(local_row, 64)
+    low = local_row - high * 64
+    coded = jnp.concatenate([hits * high.astype(F32), hits * low.astype(F32)], axis=0).astype(BF16)
+    lane = rank + lax.rem(me, in_group) * per_peer
+    spread = jnp.where(lax.broadcasted_iota(jnp.int32, (GROUP, rows_dev), 0) == lane, 1.0, 0.0).astype(BF16)
+    sent_ids = lax.dot_general(coded, spread, (((1,), (1,)), ((), ())), preferred_element_type=F32)
+    sent_ids = (sent_ids[:D] * 64.0 + sent_ids[D:]).astype(jnp.int32)
+    for t in range(D):
+        ids_s[t] = sent_ids[t:t + 1]
+    rank_ref[...] = place
+
+    pl.semaphore_wait(barrier, D - 1)
+
+    def row_copy(t, slot):
+        return pltpu.make_async_remote_copy(
+            src_ref=bs.at[t], dst_ref=rv.at[slot], send_sem=s_send.at[t], recv_sem=s_recv.at[slot],
+            device_id=(lax.div(t, C), lax.rem(t, C)), device_id_type=MESH)
+
+    def id_copy(t, slot):
+        return pltpu.make_async_remote_copy(
+            src_ref=ids_s.at[t], dst_ref=ids_r.at[slot], send_sem=i_send.at[t], recv_sem=i_recv.at[slot],
+            device_id=(lax.div(t, C), lax.rem(t, C)), device_id_type=MESH)
+
+    own_rows = pltpu.make_async_copy(bs.at[me], rv.at[me], self_sem.at[0])
+    own_ids = pltpu.make_async_copy(ids_s.at[me], ids_r.at[me], self_sem.at[1])
+
+    def send_group(i, _):
+        g = jnp.where(i < 2, i, 2 + lax.rem(i + row, R - 2))
+        slots = lax.broadcasted_iota(jnp.int32, (C * per_peer, rows_dev), 0) + g * (C * per_peer)
+        pick = jnp.where(slots == rank_ref[...], 1.0, 0.0).astype(BF16)
+        picked = dot(pick, b_ref[...]).astype(BF16)
+        bs[pl.ds(g * C, C)] = picked.reshape(C, per_peer, draws)
+
+        def send(j, _):
+            t = g * C + lax.rem(col + j, C)
+
+            @pl.when(t != me)
+            def _():
+                id_copy(t, me).start()
+                row_copy(t, me).start()
+
+            @pl.when(t == me)
+            def _():
+                own_ids.start()
+                own_rows.start()
+
+            return 0
+
+        lax.fori_loop(0, C, send, 0)
+        return 0
+
+    lax.fori_loop(0, R, send_group, 0)
+
+    def wait_arrived():
+        def wait_one(i, _):
+            s = lax.rem(me + i, D)
+            id_copy(s, s).wait_recv()
+            row_copy(s, s).wait_recv()
+            return 0
+
+        lax.fori_loop(1, D, wait_one, 0)
+        own_ids.wait()
+        own_rows.wait()
+        for g in range(groups):
+            ids_g = ids_r[g * in_group]
+            for i in range(1, in_group):
+                ids_g = ids_g + ids_r[g * in_group + i]
+            lr_ref[:, g * GROUP:(g + 1) * GROUP] = ids_g
+
+    def placed(first, count):
+        slots = lax.broadcasted_iota(jnp.int32, (count, rows_dev), 0) + first
+        put = jnp.where(slots == lr_ref[...], 1.0, 0.0).astype(BF16)
+        return dot(put, rv[...].reshape(rows_dev, draws))
+
+    def piece(k, c, q, send_sem, to_row, to_col):
+        return pltpu.make_async_remote_copy(
+            src_ref=H.at[k, c, q], dst_ref=H.at[k, c, q], send_sem=send_sem, recv_sem=p_recv.at[k, c, q],
+            device_id=(to_row, to_col), device_id_type=MESH)
+
+    def slab(k, c):
+        return pltpu.make_async_remote_copy(
+            src_ref=H.at[k, c], dst_ref=H.at[k, c], send_sem=d_send.at[c], recv_sem=d_recv.at[k, c],
+            device_id=(sibling, col), device_id_type=MESH)
+
+    def share(k):
+        @pl.when(row == k)
+        def _():
+            for q in range(1, nq):
+                piece(k, col, q, a_send.at[q], 2 * q + k, col).start()
+
+        @pl.when(core == k)
+        def _():
+            @pl.when(row != k)
+            def _():
+                piece(k, col, quarter, a_send.at[0], sibling, col).wait_recv()
+
+            for i in range(1, C):
+                other = lax.rem(col + i, C)
+                piece(k, col, quarter, b_send.at[i], row, other).start()
+            for i in range(C):
+                c = lax.rem(col + i, C)
+                if i:
+                    piece(k, c, quarter, b_send.at[i], sibling, col).wait_recv()
+                for j in range(1, nq):
+                    q = lax.rem(quarter + j, nq)
+
+                    def go(c=c, q=q, i=i, j=j):
+                        piece(k, c, quarter, c_send.at[i, j], 2 * q + k, col).start()
+
+                    if i:
+                        go()
+                    else:
+                        pl.when(q != 0)(go)
+            for i in range(C):
+                c = lax.rem(col + i, C)
+                for j in range(1, nq):
+                    q = lax.rem(quarter + j, nq)
+
+                    def take(c=c, q=q):
+                        piece(k, c, q, a_send.at[0], sibling, col).wait_recv()
+
+                    if i:
+                        take()
+                    else:
+                        pl.when(row != k)(take)
+                slab(k, c).start()
+
+        @pl.when(core != k)
+        def _():
+            for c in range(C):
+                slab(k, c).wait_recv()
+
+    def settle(k):
+        @pl.when(row == k)
+        def _():
+            for q in range(1, nq):
+                piece(k, col, q, a_send.at[q], 2 * q + k, col).wait_send()
+
+        @pl.when(core == k)
+        def _():
+            for i in range(1, C):
+                piece(k, col, quarter, b_send.at[i], row, col).wait_send()
+            for i in range(C):
+                for j in range(1, nq):
+                    q = lax.rem(quarter + j, nq)
+
+                    def done(i=i, j=j):
+                        piece(k, col, quarter, c_send.at[i, j], sibling, col).wait_send()
+
+                    if i:
+                        done()
+                    else:
+                        pl.when(q != 0)(done)
+                slab(k, lax.rem(col + i, C)).wait_send()
+
+    def solve(k):
+        whole = H[k].reshape(panel_width, draws)
+
+        def step(i, _):
+            at = pl.ds(pl.multiple_of(i * GROUP, GROUP), GROUP)
+            sol[k, at, :] = dot(dg[k, at, :], whole).astype(BF16)
+            return 0
+
+        lax.fori_loop(0, panel_width // GROUP, step, 0)
+
+    @pl.when(row < 2)
+    def _():
+        wait_arrived()
+
+    @pl.when(row == 0)
+    def _():
+        H[0, col] = placed(0, block_rows).astype(BF16).reshape(nq, sub, draws)
+
+    share(0)
+    diag_copy.wait()
+    solve(0)
+    pan_copy.wait()
+
+    @pl.when(row == 1)
+    def _():
+        second = placed(0, block_rows) - dot(pan[0, 0], sol[0])
+        H[1, col] = second.astype(BF16).reshape(nq, sub, draws)
+
+    share(1)
+    solve(1)
+
+    def trailing(i, _):
+        acc[i] = dot(pan[0, i], sol[0]) + dot(pan[1, i], sol[1])
+        return 0
+
+    lax.fori_loop(0, L, trailing, 0)
+
+    @pl.when(row >= 2)
+    def _():
+        wait_arrived()
+
+    def finish(i, _):
+        out_ref[i] = (placed(i * block_rows, block_rows) - acc[i]).astype(BF16)
+        return 0
+
+    lax.fori_loop(0, L, finish, 0)
+    own = pl.ds(pl.multiple_of(col * block_rows, block_rows), block_rows)
+    for k in range(2):
+        @pl.when(row == k)
+        def _(k=k):
+            out_ref[0] = sol[k, own, :]
+
+    def sent(i, _):
+        t = lax.rem(me + i, D)
+        id_copy(t, me).wait_send()
+        row_copy(t, me).wait_send()
+        return 0
+
+    lax.fori_loop(1, D, sent, 0)
+    settle(0)
+    settle(1)
+
+
+def kernel_per_device(b_ingest, source_point, panels, diag_inverse):
+    R, C = lax.axis_size("row"), lax.axis_size("col")
+    D = R * C
+    _, L, _, block_rows, panel_width = panels.shape
+    rows_dev, draws = b_ingest.shape
+    per_peer = rows_dev // D
+    nq = R // 2
+    dma = pltpu.SemaphoreType.DMA
+    vmem = pl.BlockSpec(memory_space=pltpu.VMEM)
+    hbm = pl.BlockSpec(memory_space=pl.ANY)
+    out = pl.pallas_call(
+        functools.partial(kernel, R, C, panel_width),
+        out_shape=jax.ShapeDtypeStruct((L, block_rows, draws), BF16),
+        in_specs=[vmem, vmem, hbm, hbm],
+        out_specs=vmem,
+        scratch_shapes=[
+            pltpu.VMEM((D, per_peer, draws), BF16),
+            pltpu.VMEM((D, per_peer, draws), BF16),
+            pltpu.VMEM((D, 1, GROUP), jnp.int32),
+            pltpu.VMEM((D, 1, GROUP), jnp.int32),
+            pltpu.VMEM((1, rows_dev), jnp.int32),
+            pltpu.VMEM((1, rows_dev), jnp.int32),
+            pltpu.VMEM((2, L, block_rows, panel_width), BF16),
+            pltpu.VMEM((2, panel_width, panel_width), BF16),
+            pltpu.VMEM((2, C, nq, block_rows // nq, draws), BF16),
+            pltpu.VMEM((2, panel_width, draws), BF16),
+            pltpu.VMEM((L, block_rows, draws), F32),
+            dma((2,)),
+            dma((2,)),
+            dma((D,)),
+            dma((D,)),
+            dma((D,)),
+            dma((D,)),
+            dma((nq,)),
+            dma((C,)),
+            dma((C, nq)),
+            dma((C,)),
+            dma((2, C, nq)),
+            dma((2, C)),
+        ],
+        compiler_params=pltpu.CompilerParams(
+            collective_id=0, has_side_effects=True, vmem_limit_bytes=60 * 1024 * 1024
+        ),
+        cost_estimate=pl.CostEstimate(
+            flops=4 * rows_dev * panel_width * draws * 2, bytes_accessed=20 * 1024 * 1024, transcendentals=0
+        ),
+    )(source_point.reshape(1, rows_dev), b_ingest, panels, diag_inverse)
+    return out.reshape(L, 1, block_rows, draws)
+
+
+def per_device(b_ingest, source_point, panels, diag_inverse):
+    R, C = lax.axis_size("row"), lax.axis_size("col")
+    rows_dev, draws = b_ingest.shape
+    block_rows, panel_width = panels.shape[3:]
+    per_peer = rows_dev // (R * C)
+    fits = (
+        R % 2 == 0 and R > 3 and C > 1
+        and per_peer % 16 == 0 and GROUP % per_peer == 0
+        and rows_dev % GROUP == 0 and panel_width % GROUP == 0
+        and block_rows % (R // 2 * 16) == 0 and rows_dev <= 64 * 256
+        and rows_dev * (12 * draws + 4 * panel_width) + panel_width * (4 * panel_width + 8 * draws) <= 48 * 1024 * 1024
+    )
+    body = kernel_per_device if fits else plain_per_device
+    return body(b_ingest, source_point, panels, diag_inverse)
+
+
 def solution(mesh):
     return jax.shard_map(
         per_device,

time: 396 us -> 187 us (0.47)
  waiting for transfers between devices: 285 us -> 0 us
  Pallas kernels: 0 us -> 180 us
  local copies, waits for them, and re-layouts: 50.6 us -> 4.64 us
  matrix products: 18.9 us -> 0 us
  between operations: 13.3 us -> 0.01 us
  starting transfers between devices: 12.6 us -> 0 us
  other arithmetic: 12.1 us -> 0 us
    pallas_call x0 -> x1, Pallas kernels: none -> 180 us  [kernel_per_device(): pl.pallas_call(functools.partial(kernel, R, C, panel_width), out_shape=ja...]
    psum x2 -> x0, waiting for transfers between devices: 106 us -> none  [broadcast(): return lax.psum(block, axis)]
    all_to_all x2 -> x0, waiting for transfers between devices: 91 us -> none  [the longest x1 91 us: per_device(): lax.all_to_all(ordered.reshape(dev_count, per_peer, draw_count), ('row',...]
    all_gather x2 -> x0, waiting for transfers between devices: 87.4 us -> none  [per_device(): lax.all_gather(shared, 'col', axis=0, tiled=True)]
    gather x2 -> x0, local copies, waits for them, and re-layouts: 25.4 us -> none  [the longest x1 13.7 us: per_device(): ordered = b_ingest[ordering]]
    dot_general x4 -> x0, matrix products: 18.9 us -> none  [the longest x2 9.48 us: per_device(): jnp.dot(factor_rows, full_solved, preferred_element_type=jnp.float32)]
    scatter x1 -> x0, local copies, waits for them, and re-layouts: 13.1 us -> none  [per_device(): jnp.zeros((rows_dev, draw_count), jnp.bfloat16).at[local_row].set(arrived)]
    all_to_all x2 -> x0, starting transfers between devices: 12.2 us -> none  [the longest x1 6.33 us: per_device(): lax.all_to_all(ordered_ids.reshape(dev_count, per_peer), ('row', 'col'),...]
  transfers between devices with their start and end apart: 6 -> 0, of which waited for: 5 -> 0; matrix products, arithmetic and copies ran while one was open for 5% -> 0% of each run, Pallas kernels for 0% -> 0%
where the time goes in v1:
time: 187 us; the launch traced here: 184 us
  Pallas kernels  180 us (96%)
  local copies, waits for them, and re-layouts  4.64 us (2%)
    pallas_call x1, Pallas kernels, kernel_per_device(): pl.pallas_call(functools.partial(kernel, R, C, panel_width), out_shape=ja...  180 us
    unnamed x1, local copies, waits for them, and re-layouts  4.64 us

profile of v1, /device:TPU:11, one launch (start us, length us, event | category | flops | bytes accessed | tf_op | source)
XLA Modules:
  0.0 184.4 jit_solution(9675604378389955762)
XLA Ops:
  0.0 179.8 %shard_map.46 = bf16[8,256,1024]{2,1,0:T(8,128)(2,1)} custom-call(s32[1,2048]{1,0:T(1,128)} %bitcast.5, bf16[2048,1024]{1,0:T(8,128)(2,1)} %b_ref.1, bf16[2,8,1,256,1024]{4,3,2,1,0:T(8,128)(2,1)} %pan_hbm.1, bf16[2,1024,1024]{2,1,0:T(8,128)(2,1)} %diag_hbm.1), custom_call_target="tpu_custom_call" | custom-call | flops 17179869184 | bytes 20971520 | tf_op jit(solution)/shard_map/pallas_call | solution.py:371
  179.8 4.6 %copy.7 = bf16[8,1,256,1024]{3,2,1,0:T(8,128)(2,1)} copy(bf16[8,1,256,1024]{3,2,1,0:T(8,128)(2,1)} %bitcast.4) | data formatting | bytes 8388608

commit v2 on v1

--- a/solution.py
+++ b/solution.py
@@ -81,13 +81,16 @@
     return result.reshape(local_count, 1, block_rows, draw_count)
 
 
+PLAN = (0, 8, 4)
+
+
 def dot(a, b):
     return jnp.dot(a, b, preferred_element_type=F32)
 
 
 def kernel(
-    R, C, panel_width, id_ref, b_ref, pan_hbm, diag_hbm, out_ref,
-    bs, rv, ids_s, ids_r, rank_ref, lr_ref, pan, dg, H, sol, acc,
+    R, C, panel_width, plan, id_ref, b_ref, pan_hbm, diag_hbm, out_ref,
+    bs, rv, ids_s, ids_r, rank_ref, lr_ref, pan, dg, H, sol, sec, fac, acc,
     local_sem, self_sem, s_send, s_recv, i_send, i_recv, a_send, b_send, c_send, d_send, p_recv, d_recv,
 ):
     D = R * C
@@ -166,32 +169,37 @@
     own_rows = pltpu.make_async_copy(bs.at[me], rv.at[me], self_sem.at[0])
     own_ids = pltpu.make_async_copy(ids_s.at[me], ids_r.at[me], self_sem.at[1])
 
-    def send_group(i, _):
-        g = jnp.where(i < 2, i, 2 + lax.rem(i + row, R - 2))
+    def group_of(i):
+        return jnp.where(i < 2, i, 2 + lax.rem(i + row, R - 2))
+
+    def pick_group(i, _):
+        g = group_of(i)
         slots = lax.broadcasted_iota(jnp.int32, (C * per_peer, rows_dev), 0) + g * (C * per_peer)
         pick = jnp.where(slots == rank_ref[...], 1.0, 0.0).astype(BF16)
         picked = dot(pick, b_ref[...]).astype(BF16)
         bs[pl.ds(g * C, C)] = picked.reshape(C, per_peer, draws)
-
-        def send(j, _):
-            t = g * C + lax.rem(col + j, C)
-
-            @pl.when(t != me)
-            def _():
-                id_copy(t, me).start()
-                row_copy(t, me).start()
-
-            @pl.when(t == me)
-            def _():
-                own_ids.start()
-                own_rows.start()
-
-            return 0
-
-        lax.fori_loop(0, C, send, 0)
-        return 0
-
-    lax.fori_loop(0, R, send_group, 0)
+        return 0
+
+    def send_one(n, _):
+        t = group_of(lax.div(n, C)) * C + lax.rem(col + n, C)
+
+        @pl.when(t != me)
+        def _():
+            id_copy(t, me).start()
+            row_copy(t, me).start()
+
+        @pl.when(t == me)
+        def _():
+            own_ids.start()
+            own_rows.start()
+
+        return 0
+
+    def send_until(first, last):
+        last = min(last, D)
+        if first < last:
+            lax.fori_loop(first, last, send_one, 0)
+        return max(first, last)
 
     def wait_arrived():
         def wait_one(i, _):
@@ -214,117 +222,150 @@
         put = jnp.where(slots == lr_ref[...], 1.0, 0.0).astype(BF16)
         return dot(put, rv[...].reshape(rows_dev, draws))
 
-    def piece(k, c, q, send_sem, to_row, to_col):
+    def piece(slot, c, q, send_sem, to_row, to_col):
         return pltpu.make_async_remote_copy(
-            src_ref=H.at[k, c, q], dst_ref=H.at[k, c, q], send_sem=send_sem, recv_sem=p_recv.at[k, c, q],
+            src_ref=H.at[slot, c, q], dst_ref=H.at[slot, c, q], send_sem=send_sem, recv_sem=p_recv.at[slot, c, q],
             device_id=(to_row, to_col), device_id_type=MESH)
 
-    def slab(k, c):
+    def slab(u, slot, c, i):
         return pltpu.make_async_remote_copy(
-            src_ref=H.at[k, c], dst_ref=H.at[k, c], send_sem=d_send.at[c], recv_sem=d_recv.at[k, c],
+            src_ref=H.at[slot, c], dst_ref=H.at[slot, c], send_sem=d_send.at[u, i], recv_sem=d_recv.at[slot, c],
             device_id=(sibling, col), device_id_type=MESH)
 
-    def share(k):
+    def share_out(u, slot, k):
+        for q in range(1, nq):
+            piece(slot, col, q, a_send.at[u, q], 2 * q + k, col).start()
+
+    def share(u, slot, k, between):
+        @pl.when(row != k)
+        def _():
+            piece(slot, col, quarter, a_send.at[u, 0], sibling, col).wait_recv()
+
+        for i in range(1, C):
+            other = lax.rem(col + i, C)
+            piece(slot, col, quarter, b_send.at[u, i], row, other).start()
+        for i in range(C):
+            c = lax.rem(col + i, C)
+            if i:
+                piece(slot, c, quarter, b_send.at[u, i], sibling, col).wait_recv()
+            for j in range(1, nq):
+                q = lax.rem(quarter + j, nq)
+
+                def go(c=c, q=q, i=i, j=j):
+                    piece(slot, c, quarter, c_send.at[u, i, j], 2 * q + k, col).start()
+
+                if i:
+                    go()
+                else:
+                    pl.when(q != 0)(go)
+            between()
+        for i in range(C):
+            c = lax.rem(col + i, C)
+            for j in range(1, nq):
+                q = lax.rem(quarter + j, nq)
+
+                def take(c=c, q=q):
+                    piece(slot, c, q, a_send.at[u, 0], sibling, col).wait_recv()
+
+                if i:
+                    take()
+                else:
+                    pl.when(row != k)(take)
+            slab(u, slot, c, i).start()
+            between()
+
+    def received(slot):
+        for c in range(C):
+            slab(0, slot, c, 0).wait_recv()
+
+    def settle(u, slot, k):
         @pl.when(row == k)
         def _():
             for q in range(1, nq):
-                piece(k, col, q, a_send.at[q], 2 * q + k, col).start()
-
-        @pl.when(core == k)
-        def _():
-            @pl.when(row != k)
-            def _():
-                piece(k, col, quarter, a_send.at[0], sibling, col).wait_recv()
-
-            for i in range(1, C):
-                other = lax.rem(col + i, C)
-                piece(k, col, quarter, b_send.at[i], row, other).start()
-            for i in range(C):
-                c = lax.rem(col + i, C)
+                piece(slot, col, q, a_send.at[u, q], 2 * q + k, col).wait_send()
+
+        for i in range(1, C):
+            piece(slot, col, quarter, b_send.at[u, i], row, col).wait_send()
+        for i in range(C):
+            for j in range(1, nq):
+                q = lax.rem(quarter + j, nq)
+
+                def done(i=i, j=j):
+                    piece(slot, col, quarter, c_send.at[u, i, j], sibling, col).wait_send()
+
                 if i:
-                    piece(k, c, quarter, b_send.at[i], sibling, col).wait_recv()
-                for j in range(1, nq):
-                    q = lax.rem(quarter + j, nq)
-
-                    def go(c=c, q=q, i=i, j=j):
-                        piece(k, c, quarter, c_send.at[i, j], 2 * q + k, col).start()
-
-                    if i:
-                        go()
-                    else:
-                        pl.when(q != 0)(go)
-            for i in range(C):
-                c = lax.rem(col + i, C)
-                for j in range(1, nq):
-                    q = lax.rem(quarter + j, nq)
-
-                    def take(c=c, q=q):
-                        piece(k, c, q, a_send.at[0], sibling, col).wait_recv()
-
-                    if i:
-                        take()
-                    else:
-                        pl.when(row != k)(take)
-                slab(k, c).start()
-
-        @pl.when(core != k)
-        def _():
-            for c in range(C):
-                slab(k, c).wait_recv()
-
-    def settle(k):
-        @pl.when(row == k)
-        def _():
-            for q in range(1, nq):
-                piece(k, col, q, a_send.at[q], 2 * q + k, col).wait_send()
-
-        @pl.when(core == k)
-        def _():
-            for i in range(1, C):
-                piece(k, col, quarter, b_send.at[i], row, col).wait_send()
-            for i in range(C):
-                for j in range(1, nq):
-                    q = lax.rem(quarter + j, nq)
-
-                    def done(i=i, j=j):
-                        piece(k, col, quarter, c_send.at[i, j], sibling, col).wait_send()
-
-                    if i:
-                        done()
-                    else:
-                        pl.when(q != 0)(done)
-                slab(k, lax.rem(col + i, C)).wait_send()
-
-    def solve(k):
-        whole = H[k].reshape(panel_width, draws)
-
+                    done()
+                else:
+                    pl.when(q != 0)(done)
+            slab(u, slot, lax.rem(col + i, C), i).wait_send()
+
+    def multiply(left, right, store):
         def step(i, _):
             at = pl.ds(pl.multiple_of(i * GROUP, GROUP), GROUP)
-            sol[k, at, :] = dot(dg[k, at, :], whole).astype(BF16)
+            store(at, dot(left(at), right))
             return 0
 
         lax.fori_loop(0, panel_width // GROUP, step, 0)
 
+    lead, early, each = plan
+    pan_copy.wait()
+
+    @pl.when(row == 1)
+    def _():
+        H[2, col] = pan[0, 0].reshape(nq, sub, draws)
+        share_out(0, 2, 1)
+
+    lax.fori_loop(0, 1, pick_group, 0)
+    sent = send_until(0, C)
+    lax.fori_loop(1, 2, pick_group, 0)
+    sent = send_until(sent, 2 * C)
+    lax.fori_loop(2, R, pick_group, 0)
+    sent = send_until(sent, sent + lead)
+
+    @pl.when(core == 1)
+    def _():
+        share(0, 2, 1, lambda: None)
+
+    sent = send_until(sent, sent + early)
+
     @pl.when(row < 2)
     def _():
         wait_arrived()
-
-    @pl.when(row == 0)
-    def _():
-        H[0, col] = placed(0, block_rows).astype(BF16).reshape(nq, sub, draws)
-
-    share(0)
+        H[core, col] = placed(0, block_rows).astype(BF16).reshape(nq, sub, draws)
+        share_out(1, core, core)
+
+    count = [sent]
+
+    def more():
+        count[0] = send_until(count[0], count[0] + each)
+
+    share(1, core, core, more)
+    sent = send_until(count[0], D)
     diag_copy.wait()
-    solve(0)
-    pan_copy.wait()
-
-    @pl.when(row == 1)
-    def _():
-        second = placed(0, block_rows) - dot(pan[0, 0], sol[0])
-        H[1, col] = second.astype(BF16).reshape(nq, sub, draws)
-
-    share(1)
-    solve(1)
+
+    @pl.when(core == 1)
+    def _():
+        received(0)
+
+    def keep(k):
+        def store(at, value):
+            sol[k, at, :] = value.astype(BF16)
+        return store
+
+    def store_second(at, value):
+        sec[at, :] = (sec[at, :].astype(F32) - value).astype(BF16)
+
+    multiply(lambda at: dg[0, at, :], H[0].reshape(panel_width, draws), keep(0))
+
+    @pl.when(core == 0)
+    def _():
+        received(2)
+        received(1)
+
+    sec[...] = H[1].reshape(panel_width, draws)
+    fac[...] = H[2].reshape(panel_width, draws)
+    multiply(lambda at: fac[at, :], sol[0], store_second)
+    multiply(lambda at: dg[1, at, :], sec[...], keep(1))
 
     def trailing(i, _):
         acc[i] = dot(pan[0, i], sol[0]) + dot(pan[1, i], sol[1])
@@ -347,15 +388,19 @@
         def _(k=k):
             out_ref[0] = sol[k, own, :]
 
-    def sent(i, _):
+    def left(i, _):
         t = lax.rem(me + i, D)
         id_copy(t, me).wait_send()
         row_copy(t, me).wait_send()
         return 0
 
-    lax.fori_loop(1, D, sent, 0)
-    settle(0)
-    settle(1)
+    lax.fori_loop(1, D, left, 0)
+
+    @pl.when(core == 1)
+    def _():
+        settle(0, 2, 1)
+
+    settle(1, core, core)
 
 
 def kernel_per_device(b_ingest, source_point, panels, diag_inverse):
@@ -369,7 +414,7 @@
     vmem = pl.BlockSpec(memory_space=pltpu.VMEM)
     hbm = pl.BlockSpec(memory_space=pl.ANY)
     out = pl.pallas_call(
-        functools.partial(kernel, R, C, panel_width),
+        functools.partial(kernel, R, C, panel_width, PLAN),
         out_shape=jax.ShapeDtypeStruct((L, block_rows, draws), BF16),
         in_specs=[vmem, vmem, hbm, hbm],
         out_specs=vmem,
@@ -382,8 +427,10 @@
             pltpu.VMEM((1, rows_dev), jnp.int32),
             pltpu.VMEM((2, L, block_rows, panel_width), BF16),
             pltpu.VMEM((2, panel_width, panel_width), BF16),
-            pltpu.VMEM((2, C, nq, block_rows // nq, draws), BF16),
+            pltpu.VMEM((3, C, nq, block_rows // nq, draws), BF16),
             pltpu.VMEM((2, panel_width, draws), BF16),
+            pltpu.VMEM((panel_width, draws), BF16),
+            pltpu.VMEM((panel_width, panel_width), BF16),
             pltpu.VMEM((L, block_rows, draws), F32),
             dma((2,)),
             dma((2,)),
@@ -391,12 +438,12 @@
             dma((D,)),
             dma((D,)),
             dma((D,)),
-            dma((nq,)),
-            dma((C,)),
-            dma((C, nq)),
-            dma((C,)),
+            dma((2, nq)),
+            dma((2, C)),
             dma((2, C, nq)),
             dma((2, C)),
+            dma((3, C, nq)),
+            dma((3, C)),
         ],
         compiler_params=pltpu.CompilerParams(
             collective_id=0, has_side_effects=True, vmem_limit_bytes=60 * 1024 * 1024
@@ -414,11 +461,11 @@
     block_rows, panel_width = panels.shape[3:]
     per_peer = rows_dev // (R * C)
     fits = (
-        R % 2 == 0 and R > 3 and C > 1
+        R % 2 == 0 and R > 3 and C > 1 and panel_width == draws
         and per_peer % 16 == 0 and GROUP % per_peer == 0
         and rows_dev % GROUP == 0 and panel_width % GROUP == 0
         and block_rows % (R // 2 * 16) == 0 and rows_dev <= 64 * 256
-        and rows_dev * (12 * draws + 4 * panel_width) + panel_width * (4 * panel_width + 8 * draws) <= 48 * 1024 * 1024
+        and rows_dev * (12 * draws + 4 * panel_width) + panel_width * (6 * panel_width + 12 * draws) <= 50 * 1024 * 1024
     )
     body = kernel_per_device if fits else plain_per_device
     return body(b_ingest, source_point, panels, diag_inverse)

time: 187 us -> 171 us (0.914); the launches traced: 184 us -> 171 us
  Pallas kernels: 180 us -> 166 us
    pallas_call x1, Pallas kernels: 180 us -> 166 us  [kernel_per_device(): pl.pallas_call(functools.partial(kernel, R, C, panel_width, PLAN), out_sh...]
where the time goes in v2:
time: 171 us
  Pallas kernels  166 us (97%)
  local copies, waits for them, and re-layouts  4.64 us (3%)
    pallas_call x1, Pallas kernels, kernel_per_device(): pl.pallas_call(functools.partial(kernel, R, C, panel_width, PLAN), out_sh...  166 us
    unnamed x1, local copies, waits for them, and re-layouts  4.64 us

profile of v2, /device:TPU:11, one launch (start us, length us, event | category | flops | bytes accessed | tf_op | source)
XLA Modules:
  0.0 170.6 jit_solution(1514452610300682236)
XLA Ops:
  0.0 166.0 %shard_map.46 = bf16[8,256,1024]{2,1,0:T(8,128)(2,1)} custom-call(s32[1,2048]{1,0:T(1,128)} %bitcast.5, bf16[2048,1024]{1,0:T(8,128)(2,1)} %b_ref.1, bf16[2,8,1,256,1024]{4,3,2,1,0:T(8,128)(2,1)} %pan_hbm.1, bf16[2,1024,1024]{2,1,0:T(8,128)(2,1)} %diag_hbm.1), custom_call_target="tpu_custom_call" | custom-call | flops 17179869184 | bytes 20971520 | tf_op jit(solution)/shard_map/pallas_call | solution.py:416
  166.0 4.6 %copy.7 = bf16[8,1,256,1024]{3,2,1,0:T(8,128)(2,1)} copy(bf16[8,1,256,1024]{3,2,1,0:T(8,128)(2,1)} %bitcast.4) | data formatting | bytes 8388608

commit v3 on v2

--- a/solution.py
+++ b/solution.py
@@ -357,6 +357,12 @@
 
     multiply(lambda at: dg[0, at, :], H[0].reshape(panel_width, draws), keep(0))
 
+    def first_panel(i, _):
+        acc[i] = dot(pan[0, i], sol[0])
+        return 0
+
+    lax.fori_loop(0, L, first_panel, 0)
+
     @pl.when(core == 0)
     def _():
         received(2)
@@ -367,11 +373,11 @@
     multiply(lambda at: fac[at, :], sol[0], store_second)
     multiply(lambda at: dg[1, at, :], sec[...], keep(1))
 
-    def trailing(i, _):
-        acc[i] = dot(pan[0, i], sol[0]) + dot(pan[1, i], sol[1])
-        return 0
-
-    lax.fori_loop(0, L, trailing, 0)
+    def second_panel(i, _):
+        acc[i] += dot(pan[1, i], sol[1])
+        return 0
+
+    lax.fori_loop(0, L, second_panel, 0)
 
     @pl.when(row >= 2)
     def _():

time: 171 us -> 172 us (level)
  no operation moved by 1% of the time
where the time goes in v3:
time: 172 us
  Pallas kernels  167 us (97%)
  local copies, waits for them, and re-layouts  4.64 us (3%)
    pallas_call x1, Pallas kernels, kernel_per_device(): pl.pallas_call(functools.partial(kernel, R, C, panel_width, PLAN), out_sh...  167 us
    unnamed x1, local copies, waits for them, and re-layouts  4.64 us

profile of v3, /device:TPU:11, one launch (start us, length us, event | category | flops | bytes accessed | tf_op | source)
XLA Modules:
  0.0 172.0 jit_solution(12516669283406556836)
XLA Ops:
  0.0 167.4 %shard_map.46 = bf16[8,256,1024]{2,1,0:T(8,128)(2,1)} custom-call(s32[1,2048]{1,0:T(1,128)} %bitcast.5, bf16[2048,1024]{1,0:T(8,128)(2,1)} %b_ref.1, bf16[2,8,1,256,1024]{4,3,2,1,0:T(8,128)(2,1)} %pan_hbm.1, bf16[2,1024,1024]{2,1,0:T(8,128)(2,1)} %diag_hbm.1), custom_call_target="tpu_custom_call" | custom-call | flops 17179869184 | bytes 20971520 | tf_op jit(solution)/shard_map/pallas_call | solution.py:422
  167.4 4.6 %copy.7 = bf16[8,1,256,1024]{3,2,1,0:T(8,128)(2,1)} copy(bf16[8,1,256,1024]{3,2,1,0:T(8,128)(2,1)} %bitcast.4) | data formatting | bytes 8388608
